TPU v7x, 32 devices: a whole 2x2x4 slice. The times are simulated.
32 devices in a mesh: leaf: 4 (over y, x), owner: 8 (over z, core).
Axes of the slice: x: 2, y: 2, z: 4, core: 2. Of those that a mesh axis runs over, the one named last changes fastest.
Arguments:
- multipoles: float32 [3, 343, 12288], P(None, None, ('leaf', 'owner')), may hold values from -6 to 6
- operators: bfloat16 [4, 1029, 1029], replicated, may hold values from -0.1875 to 0.1875
- lists: int32 [12288, 4], P(('leaf', 'owner')), may hold values from -1 to 447, as said below
- send_slots: int32 [32, 8, 4], P(('leaf', 'owner')), may hold values from -1 to 31, as said below
Outputs:
- locals_out: float32 [3, 343, 12288], P(None, None, ('leaf', 'owner'))
Inputs may be any that keep to these rules, and one draw needn't show every extreme that they name: `lists`: A code of the first kind appears only for boxes of groups other than the first, of the third kind only for groups other than the last; a code naming (p, c) appears only where send_slots of owner p for this owner holds a slot at c, and never with p equal to the box's own owner. `send_slots`: entries are distinct boundary slots followed by -1 padding; the entries for an owner itself are all -1; every draw fills some pair's 4 entries.
All inputs are finite; a program needn't handle non-finite values.
Results may differ from a plain program's by a relative error of at most 0.0029.
Values may be sent and summed in bfloat16 or wider, within the bound.
A program may use at most 128 MiB of HBM per device.

v0:
```python
import jax
import jax.numpy as jnp
from jax import lax
from jax.sharding import PartitionSpec as P

DIRS = 4
FACE = 16
BOUND = 32


def with_halo(block, sides, width):
    for axis, dim in sides:
        count = lax.axis_size(axis)
        forward = [(i, i + 1) for i in range(count - 1)]
        backward = [(target, source) for source, target in forward]
        low = lax.ppermute(
            lax.slice_in_dim(block, block.shape[dim] - width, None, axis=dim), axis, forward
        )
        high = lax.ppermute(lax.slice_in_dim(block, 0, width, axis=dim), axis, backward)
        block = jnp.concatenate([low, block, high], axis=dim)
    return block


def select_columns(source, wanted):
    positions = lax.broadcasted_iota(jnp.int32, (source.shape[1], wanted.shape[0]), 0)
    selector = (positions == wanted[None, :]).astype(jnp.bfloat16)
    return jnp.dot(source, selector, preferred_element_type=jnp.float32)


def local(multipoles, operators, lists, send_slots):
    comps, nodes, nboxes = multipoles.shape
    width = comps * nodes
    packed = multipoles.reshape(width, nboxes).astype(jnp.bfloat16)
    extended = with_halo(packed, (("leaf", 1),), FACE)
    owners = lax.axis_size("owner")
    capacity = send_slots.shape[2]
    slots = send_slots[0].reshape(-1)
    chosen = select_columns(packed[:, :BOUND], slots).astype(jnp.bfloat16)
    outgoing = chosen.reshape(width, owners, capacity)
    arrived, arrived_slots = (
        lax.all_to_all(outgoing, "owner", split_axis=1, concat_axis=1, tiled=True),
        lax.all_to_all(send_slots, "owner", split_axis=1, concat_axis=1, tiled=True),
    )
    ghost_table = arrived.reshape(width, owners * capacity)
    extent = extended.shape[1]
    total = jnp.zeros((width, nboxes), jnp.float32)
    for direction in range(DIRS):
        codes = lists[:, direction]
        near_part = select_columns(extended, codes)
        ghost_part = select_columns(ghost_table, codes - extent)
        columns = (near_part + ghost_part).astype(jnp.bfloat16)
        total = total + jnp.dot(operators[direction], columns, preferred_element_type=jnp.float32)
    return total.reshape(comps, nodes, nboxes)


def solution(mesh):
    return jax.shard_map(
        local,
        mesh=mesh,
        in_specs=(
            P(None, None, ("leaf", "owner")),
            P(),
            P(("leaf", "owner"), None),
            P(("leaf", "owner"), None, None),
        ),
        out_specs=P(None, None, ("leaf", "owner")),
        check_vma=False,
    )
```

profile of v0, /device:TPU:0, one launch (start us, length us, event | category | flops | bytes accessed | tf_op | source)
XLA Modules:
  0.0 74.4 jit_solution(971317104322656654)
XLA Ops:
  0.0 0.0 copy-start.1
  0.0 1.5 %convert_element_type.33 = bf16[3,343,384]{2,1,0:T(8,128)(2,1)S(1)} convert(f32[3,343,384]{2,1,0:T(8,128)} %param.4) | non-fusion elementwise | flops 395136 | bytes 2370816 | tf_op jit(solution)/shard_map/convert_element_type | solution.py:33
  1.5 0.0 copy-start
  1.5 0.2 convert_element_type.34
  1.7 0.0 copy-done.1
  1.7 0.1 copy.6
  1.8 0.1 eq.85
  1.9 0.2 fusion.6
  2.1 0.7 reshape.36
  2.8 6.3 %all-to-all-start = ((bf16[1029,8,4]{0,2,1:T(4,128)(2,1)}), bf16[1029,8,4]{0,2,1:T(4,128)(2,1)S(1)}, u32[]{:S(2)}, u32[]{:S(2)}) async-start(bf16[1029,8,4]{0,2,1:T(4,128)(2,1)} %reshape.36), calls=%async_computation | async-start | bytes 147456 | tf_op jit(solution)/shard_map/all_to_all | solution.py:41
  9.1 0.1 fusion.28
  9.3 3.4 %collective-permute-start = (bf16[1029,16]{1,0:T(8,128)(2,1)S(1)}, bf16[1029,16]{1,0:T(8,128)(2,1)S(1)}, u32[]{:S(2)}, u32[]{:S(2)}) collective-permute-start(bf16[1029,16]{1,0:T(8,128)(2,1)S(1)} %get-tuple-element.13), channel_id=1, source_target_pairs={{0,8},{8,16},{16,24},{1,9},{9,17},{17,25},{2,10},{10,18},{18,26},{... | collective-permute-start | bytes 98792 | tf_op jit(solution)/shard_map/ppermute | solution.py:16
  12.7 1.3 %collective-permute-start.1 = (bf16[1029,16]{1,0:T(8,128)(2,1)S(1)}, bf16[1029,16]{1,0:T(8,128)(2,1)S(1)}, u32[]{:S(2)}, u32[]{:S(2)}) collective-permute-start(bf16[1029,16]{1,0:T(8,128)(2,1)S(1)} %get-tuple-element.14), channel_id=1, source_target_pairs={{8,0},{16,8},{24,16},{9,1},{17,9},{25,17},{10,2},{18,10},{26,18},{... | collective-permute-start | bytes 98792 | tf_op jit(solution)/shard_map/ppermute | solution.py:19
  14.0 0.0 copy-done
  14.0 26.6 %fusion.27 = (bf16[1,1029,1029]{2,0,1:T(2,128)(2,1)}, bf16[1,1029,1029]{2,0,1:T(2,128)(2,1)}, bf16[1,1029,1029]{2,0,1:T(2,128)(2,1)}, bf16[1,1029,1029]{2,0,1:T(2,128)(2,1)}) fusion(bf16[4,1029,1029]{2,0,1:T(4,128)(2,1)} %param.5), kind=kLoop, calls=%fused_computation.52 | loop fusion | bytes 16941456 | tf_op jit(solution)/shard_map/slice | solution.py:52
  40.6 0.0 all-to-all-done
  40.7 1.6 %fusion.16 = f32[1029,384]{1,0:T(8,128)} fusion(bf16[1029,32]{0,1:T(8,128)(2,1)S(1)} %reshape.37, s32[384]{0:T(512)S(1)} %get-tuple-element.18), kind=kOutput, calls=%fused_computation.33 | convolution fusion | flops 25300992 | bytes 1647936 | tf_op jit(solution)/shard_map/dot_general | solution.py:27
  42.3 1.6 %fusion.17 = f32[1029,384]{1,0:T(8,128)} fusion(bf16[1029,32]{0,1:T(8,128)(2,1)S(1)} %reshape.37, s32[384]{0:T(512)S(1)} %get-tuple-element.17), kind=kOutput, calls=%fused_computation.34 | convolution fusion | flops 25300992 | bytes 1647936 | tf_op jit(solution)/shard_map/dot_general | solution.py:27
  43.9 1.6 %fusion.18 = f32[1029,384]{1,0:T(8,128)} fusion(bf16[1029,32]{0,1:T(8,128)(2,1)S(1)} %reshape.37, s32[384]{0:T(512)S(1)} %get-tuple-element.16), kind=kOutput, calls=%fused_computation.35 | convolution fusion | flops 25300992 | bytes 1647936 | tf_op jit(solution)/shard_map/dot_general | solution.py:27
  45.5 0.5 fusion.19
  45.9 0.0 collective-permute-done
  45.9 0.0 collective-permute-done.1
  46.0 6.2 %fusion.5 = f32[384,1029]{0,1:T(8,128)} fusion(bf16[1,1029,1029]{2,0,1:T(2,128)(2,1)} %get-tuple-element.12, f32[1029,384]{1,0:T(8,128)} %fusion.16, s32[384]{0:T(512)S(1)} %get-tuple-element.7, bf16[1029,16]{1,0:T(8,128)(2,1)S(1)} %collective-permute-done.1, bf16[1029,384]{1,0:T(8,128)(2,1)S(1)} %convert_element_type.34, ...), kind=kOutput, calls=%fused_computation.16 | convolution fusion | flops 1145461504 | bytes 6136434 | tf_op jit(solution)/shard_map/dot_general | solution.py:52
  52.2 6.6 %convolution_add_fusion.6 = f32[384,1029]{0,1:T(8,128)} fusion(f32[384,1029]{0,1:T(8,128)} %fusion.5, bf16[1,1029,1029]{2,0,1:T(2,128)(2,1)} %get-tuple-element.11, f32[1029,384]{1,0:T(8,128)} %fusion.17, s32[384]{0:T(512)S(1)} %get-tuple-element.6, bf16[1029,16]{1,0:T(8,128)(2,1)S(1)} %collective-permute-done.1, ...), kind=kOutput, calls=%fused_computation.6 | convolution fusion | flops 1145856640 | bytes 7716978 | tf_op jit(solution)/shard_map/dot_general | solution.py:52
  58.8 6.6 %convolution_add_fusion.5 = f32[384,1029]{0,1:T(8,128)} fusion(f32[384,1029]{0,1:T(8,128)} %convolution_add_fusion.6, bf16[1,1029,1029]{2,0,1:T(2,128)(2,1)} %get-tuple-element.10, f32[1029,384]{1,0:T(8,128)} %fusion.18, s32[384]{0:T(512)S(1)} %get-tuple-element.8, bf16[1029,16]{1,0:T(8,128)(2,1)S(1)} %collective-permute-done.1, ...), kind=kOutput, calls=%fused_computation.5 | convolution fusion | flops 1145856640 | bytes 7716978 | tf_op jit(solution)/shard_map/dot_general | solution.py:52
  65.4 6.2 %fusion = f32[1029,384]{1,0:T(8,128)} fusion(f32[384,1029]{0,1:T(8,128)} %convolution_add_fusion.5, bf16[1,1029,1029]{2,0,1:T(2,128)(2,1)} %get-tuple-element.9, f32[1029,384]{1,0:T(8,128)S(1)} %fusion.19, s32[384]{0:T(512)S(1)} %get-tuple-element.5, bf16[1029,16]{1,0:T(8,128)(2,1)S(1)} %collective-permute-done.1, ...), kind=kOutput, calls=%fused_computation.7 | convolution fusion | flops 1145856640 | bytes 7716978 | tf_op jit(solution)/shard_map/dot_general | solution.py:52
  71.6 2.7 %reshape.38 = f32[3,343,384]{2,1,0:T(8,128)} reshape(f32[1029,384]{1,0:T(8,128)} %fusion) | data formatting | bytes 3161088 | tf_op jit(solution)/shard_map/reshape | solution.py:53
  (4 shorter events, 0.1 us)
Async XLA Ops:
  0.0 1.7 %copy-start.1 = (s32[1,8,4]{1,2,0:T(4,128)S(1)}, s32[1,8,4]{1,2,0:T(4,128)}, u32[]{:S(2)}) copy-start(s32[1,8,4]{1,2,0:T(4,128)} %param.7) | copy-start | bytes 388
  1.5 12.5 %copy-start = (s32[384,4]{0,1:T(4,128)S(1)}, s32[384,4]{0,1:T(4,128)}, u32[]{:S(2)}) copy-start(s32[384,4]{0,1:T(4,128)} %param.6) | copy-start | bytes 18436
  2.8 37.8 %all-to-all-start = ((bf16[1029,8,4]{0,2,1:T(4,128)(2,1)}), bf16[1029,8,4]{0,2,1:T(4,128)(2,1)S(1)}, u32[]{:S(2)}, u32[]{:S(2)}) async-start(bf16[1029,8,4]{0,2,1:T(4,128)(2,1)} %reshape.36), calls=%async_computation | async-start | bytes 147456 | tf_op jit(solution)/shard_map/all_to_all | solution.py:41
  9.3 36.7 %collective-permute-start = (bf16[1029,16]{1,0:T(8,128)(2,1)S(1)}, bf16[1029,16]{1,0:T(8,128)(2,1)S(1)}, u32[]{:S(2)}, u32[]{:S(2)}) collective-permute-start(bf16[1029,16]{1,0:T(8,128)(2,1)S(1)} %get-tuple-element.13), channel_id=1, source_target_pairs={{0,8},{8,16},{16,24},{1,9},{9,17},{17,25},{2,10},{10,18},{18,26},{... | collective-permute-start | bytes 98792 | tf_op jit(solution)/shard_map/ppermute | solution.py:16
  12.7 33.3 %collective-permute-start.1 = (bf16[1029,16]{1,0:T(8,128)(2,1)S(1)}, bf16[1029,16]{1,0:T(8,128)(2,1)S(1)}, u32[]{:S(2)}, u32[]{:S(2)}) collective-permute-start(bf16[1029,16]{1,0:T(8,128)(2,1)S(1)} %get-tuple-element.14), channel_id=1, source_target_pairs={{8,0},{16,8},{24,16},{9,1},{17,9},{25,17},{10,2},{18,10},{26,18},{... | collective-permute-start | bytes 98792 | tf_op jit(solution)/shard_map/ppermute | solution.py:19
where the time goes:
time: 75.7 us; the launch traced here: 74.4 us
  matrix products  31.2 us (41%)
  local copies, waits for them, and re-layouts  30.5 us (40%)
  starting transfers between devices  11 us (15%)
  other arithmetic  1.52 us (2%)
    slice x1, local copies, waits for them, and re-layouts, local(): operators[direction]  26.6 us
    dot_general x4, matrix products, local(): jnp.dot(operators[direction], columns, preferred_element_type=jnp.float32)  25.7 us
    all_to_all x1, starting transfers between devices, local(): lax.all_to_all(outgoing, 'owner', split_axis=1, concat_axis=1, tiled=True)  6.33 us
    dot_general x5, matrix products, select_columns(): return jnp.dot(source, selector, preferred_element_type=jnp.float32)  5.5 us
    ppermute x1, starting transfers between devices, with_halo(): lax.ppermute(lax.slice_in_dim(block, block.shape[dim] - width, None, axis...  3.41 us
    reshape x1, local copies, waits for them, and re-layouts, local(): return total.reshape(comps, nodes, nboxes)  2.73 us
  transfers between devices with their start and end apart: 3, of which 0 were waited for; matrix products, arithmetic and copies ran while one was open for 43% of the time, Pallas kernels for 0%

commit v1 on v0

v1 whole, which is shorter than its diff:
```python
import functools

import jax
import jax.numpy as jnp
from jax import lax
from jax.experimental import pallas as pl
from jax.experimental.pallas import tpu as pltpu
from jax.sharding import PartitionSpec as P

FACE = 16
BOUND = 32
LANES = 128
F32 = jnp.float32
BF16 = jnp.bfloat16
MESH = pl.DeviceIdType.MESH


def round_up(value, unit):
    return (value + unit - 1) // unit * unit


def iota(shape, dim):
    return lax.broadcasted_iota(jnp.int32, shape, dim)


def one_hot(condition):
    return jnp.where(condition, 1.0, 0.0).astype(BF16)


def dot_nt(a, b):
    return lax.dot_general(a, b, (((1,), (1,)), ((), ())), preferred_element_type=F32)


def kernel(
    groups, owners, cap, first,
    mult, ops, lists, slots, out,
    opv, mv, packf, packed, pb, y_first, y_rest, ga, gb, face_out, face_in, ghost_out, ghost_in,
    op_sem, m_sem, face_send, face_recv, ghost_send, ghost_recv,
):
    comps, nodes, nboxes = mv.shape
    width = comps * nodes
    dirs = lists.shape[0]
    rest = nboxes - first
    span = y_first.shape[1] // dirs
    leaf = lax.axis_index("leaf")
    me = lax.axis_index("owner")

    def op_copy(c):
        rows = pl.ds(c * nodes, nodes)
        return pltpu.make_async_copy(ops.at[rows], opv.at[c, pl.ds(0, nodes)], op_sem.at[c])

    m_copy = pltpu.make_async_copy(mult, mv, m_sem)
    m_copy.start()
    for c in range(comps):
        op_copy(c).start()

    face_in[...] = jnp.zeros_like(face_in)
    ghost_in[...] = jnp.zeros_like(ghost_in)

    barrier = pltpu.get_barrier_semaphore()

    def greet(k, carry):
        peer = lax.rem(me + k, owners)
        pl.semaphore_signal(barrier, inc=1, device_id=(leaf, peer), device_id_type=MESH)
        return carry

    lax.fori_loop(1, owners, greet, 0)

    @pl.when(leaf > 0)
    def _():
        pl.semaphore_signal(barrier, inc=1, device_id=(leaf - 1, me), device_id_type=MESH)

    @pl.when(leaf < groups - 1)
    def _():
        pl.semaphore_signal(barrier, inc=1, device_id=(leaf + 1, me), device_id_type=MESH)

    rows = owners * cap
    spread = jnp.where(iota((rows, owners), 0) // cap == iota((rows, owners), 1), 1.0, 0.0)
    spread = dot_nt(spread.astype(BF16), slots[...].astype(F32).astype(BF16))
    here = iota((rows, cap), 0) % cap == iota((rows, cap), 1)
    slot = jnp.sum(jnp.where(here, spread, 0.0), axis=1, keepdims=True)
    chooser = one_hot(iota((rows, LANES), 1).astype(F32) == slot)
    low_pick = one_hot(iota((FACE, LANES), 0) == iota((FACE, LANES), 1))
    high_pick = one_hot(iota((FACE, LANES), 0) + (LANES - FACE) == iota((FACE, LANES), 1))

    m_copy.wait()
    for c in range(comps):
        packf[pl.ds(c * nodes, nodes), :] = mv[c]
    packed[...] = packf[...].astype(BF16)
    head = packed[:, :LANES]
    tail = packed[:, nboxes - LANES:]
    picked = dot_nt(jnp.concatenate([low_pick, chooser], axis=0), head)
    face_out[0] = picked[:FACE].astype(BF16)
    face_out[1] = dot_nt(high_pick, tail).astype(BF16)
    for p in range(owners):
        ghost_out[p] = picked[FACE + p * cap:FACE + (p + 1) * cap].astype(BF16)

    barrier_count = owners - 1 + jnp.where(leaf > 0, 1, 0) + jnp.where(leaf < groups - 1, 1, 0)
    pl.semaphore_wait(barrier, barrier_count)

    def face_copy(side):
        step = -1 if side == 0 else 1
        return pltpu.make_async_remote_copy(
            src_ref=face_out.at[side], dst_ref=face_in.at[1 - side],
            send_sem=face_send.at[side], recv_sem=face_recv.at[1 - side],
            device_id=(leaf + step, me), device_id_type=MESH,
        )

    def ghost_copy(k):
        peer = lax.rem(me + k, owners)
        return pltpu.make_async_remote_copy(
            src_ref=ghost_out.at[peer], dst_ref=ghost_in.at[me],
            send_sem=ghost_send.at[k], recv_sem=ghost_recv.at[k],
            device_id=(leaf, peer), device_id_type=MESH,
        )

    @pl.when(leaf > 0)
    def _():
        face_copy(0).start()

    @pl.when(leaf < groups - 1)
    def _():
        face_copy(1).start()

    lax.fori_loop(1, owners, lambda k, carry: (ghost_copy(k).start(), carry)[1], 0)

    code = lists[...]
    place = jnp.where(
        code < 0, -1,
        jnp.where(code < FACE, code + nboxes, jnp.where(code < FACE + nboxes, code - FACE, code)),
    )
    for d in range(dirs):
        row = place[d:d + 1, :]
        ga[d] = one_hot(iota((first, nboxes), 0) == row)
        gb[d] = one_hot(iota((gb.shape[1], nboxes), 0) + first == row)

    def translate(c, weights, select):
        lhs = opv[c].reshape(span * dirs, width)
        y = y_first if weights.shape[1] == first else y_rest
        product = jnp.dot(lhs, weights, preferred_element_type=F32)
        for t in range(y.shape[0]):
            y[t] = product[:, t * LANES:(t + 1) * LANES]
        total = None
        for d in range(dirs):
            part = jnp.concatenate(
                [y[t, pl.ds(d, span, stride=dirs), :].astype(BF16) for t in range(y.shape[0])],
                axis=1,
            )
            term = jnp.dot(part, select[d], preferred_element_type=F32)
            total = term if total is None else total + term
        return total[:nodes]

    def first_pass(c, carry):
        op_copy(c).wait()
        out[c] = translate(c, packed[:, :first], ga)
        return carry

    lax.fori_loop(0, comps, first_pass, 0)

    @pl.when(leaf < groups - 1)
    def _():
        face_copy(1).wait_send()
        face_copy(0).wait_recv()

    @pl.when(leaf > 0)
    def _():
        face_copy(0).wait_send()
        face_copy(1).wait_recv()

    lax.fori_loop(1, owners, lambda k, carry: (ghost_copy(k).wait(), carry)[1], 0)

    pieces = [face_in[0].astype(F32), face_in[1].astype(F32)]
    ghosts = [ghost_in[p].astype(F32) for p in range(owners)]
    table = jnp.concatenate(pieces + ghosts, axis=0)
    pad = gb.shape[1] - rest - table.shape[0]
    if pad:
        table = jnp.concatenate([table, jnp.zeros((pad, width), F32)], axis=0)
    pb[:, :rest] = packed[:, first:]
    pb[:, rest:] = table.T.astype(BF16)

    def second_pass(c, carry):
        out[c] = out[c] + translate(c, pb[...], gb)
        return carry

    lax.fori_loop(0, comps, second_pass, 0)


def local(groups, owners, multipoles, operators, lists, send_slots):
    comps, nodes, nboxes = multipoles.shape
    dirs, width, _ = operators.shape
    cap = send_slots.shape[2]
    first = nboxes // 256 * 256 if nboxes % 256 else nboxes - 256
    extra = round_up(nboxes - first + 2 * FACE + owners * cap, LANES)
    extra = max(extra, 256)
    span = round_up(nodes, 8)
    anywhere = pl.BlockSpec(memory_space=pl.ANY)
    vmem = pl.BlockSpec(memory_space=pltpu.VMEM)
    dma = pltpu.SemaphoreType.DMA
    return pl.pallas_call(
        functools.partial(kernel, groups, owners, cap, first),
        out_shape=jax.ShapeDtypeStruct((comps, nodes, nboxes), F32),
        in_specs=[anywhere, anywhere, vmem, vmem],
        out_specs=vmem,
        scratch_shapes=[
            pltpu.VMEM((comps, span, dirs, width), BF16),
            pltpu.VMEM((comps, nodes, nboxes), F32),
            pltpu.VMEM((width, nboxes), F32),
            pltpu.VMEM((width, nboxes), BF16),
            pltpu.VMEM((width, extra), BF16),
            pltpu.VMEM((first // LANES, span * dirs, LANES), F32),
            pltpu.VMEM((extra // LANES, span * dirs, LANES), F32),
            pltpu.VMEM((dirs, first, nboxes), BF16),
            pltpu.VMEM((dirs, extra, nboxes), BF16),
            pltpu.VMEM((2, FACE, width), BF16),
            pltpu.VMEM((2, FACE, width), BF16),
            pltpu.VMEM((owners, cap, width), BF16),
            pltpu.VMEM((owners, cap, width), BF16),
            dma((comps,)), dma, dma((2,)), dma((2,)), dma((owners,)), dma((owners,)),
        ],
        compiler_params=pltpu.CompilerParams(
            collective_id=0, has_side_effects=True, vmem_limit_bytes=58 << 20
        ),
        cost_estimate=pl.CostEstimate(
            flops=2 * dirs * width * width * nboxes,
            bytes_accessed=2 * dirs * width * width + 8 * width * nboxes,
            transcendentals=0,
        ),
    )(
        multipoles,
        operators.transpose(1, 0, 2),
        lists.T,
        send_slots.reshape(owners, cap).T,
    )


def solution(mesh):
    return jax.shard_map(
        functools.partial(local, mesh.shape["leaf"], mesh.shape["owner"]),
        mesh=mesh,
        in_specs=(
            P(None, None, ("leaf", "owner")),
            P(),
            P(("leaf", "owner"), None),
            P(("leaf", "owner"), None, None),
        ),
        out_specs=P(None, None, ("leaf", "owner")),
        check_vma=False,
    )
```

time: 75.7 us -> 24.2 us (0.32); the launches traced: 74.4 us -> 24 us
  matrix products: 31.2 us -> 0 us
  local copies, waits for them, and re-layouts: 30.5 us -> 2.66 us
  Pallas kernels: 0 us -> 21.3 us
  starting transfers between devices: 11 us -> 0 us
  other arithmetic: 1.52 us -> 0 us
    dot_general x9 -> x0, matrix products: 31.2 us -> none  [the longest x4 25.7 us: local(): jnp.dot(operators[direction], columns, preferred_element_type=jnp.float32)]
    slice x3 -> x0, local copies, waits for them, and re-layouts: 26.7 us -> none  [the longest x1 26.6 us: local(): operators[direction]]
    pallas_call x0 -> x1, Pallas kernels: none -> 21.3 us  [local(): pl.pallas_call(functools.partial(kernel, groups, owners, cap, first), out...]
    all_to_all x1 -> x0, starting transfers between devices: 6.33 us -> none  [local(): lax.all_to_all(outgoing, 'owner', split_axis=1, concat_axis=1, tiled=True)]
    ppermute x2 -> x0, starting transfers between devices: 4.7 us -> none  [the longest x1 3.41 us: with_halo(): lax.ppermute(lax.slice_in_dim(block, block.shape[dim] - width, None, axis...]
    reshape x3 -> x0, local copies, waits for them, and re-layouts: 3.43 us -> none  [the longest x1 2.73 us: local(): return total.reshape(comps, nodes, nboxes)]
    unnamed x5 -> x1, local copies, waits for them, and re-layouts: 0.09 us -> 2.66 us
    convert_element_type x1 -> x0, other arithmetic: 1.51 us -> none  [local(): packed = multipoles.reshape(width, nboxes).astype(jnp.bfloat16)]
  transfers between devices with their start and end apart: 3 -> 0, of which waited for: 0 -> 0; matrix products, arithmetic and copies ran while one was open for 43% -> 0% of each run, Pallas kernels for 0% -> 0%
where the time goes in v1:
time: 24.2 us; the launch traced here: 24 us
  Pallas kernels  21.3 us (88%)
  local copies, waits for them, and re-layouts  2.66 us (11%)
    pallas_call x1, Pallas kernels, local(): pl.pallas_call(functools.partial(kernel, groups, owners, cap, first), out...  21.3 us
    unnamed x1, local copies, waits for them, and re-layouts  2.66 us

profile of v1, /device:TPU:0, one launch (start us, length us, event | category | flops | bytes accessed | tf_op | source)
XLA Modules:
  0.0 24.0 jit_solution(6403733367404588090)
XLA Ops:
  0.0 21.3 %shard_map.46 = f32[3,343,384]{2,1,0:T(8,128)} custom-call(f32[3,343,384]{2,1,0:T(8,128)} %mult.1, bf16[1029,4,1029]{2,1,0:T(4,128)(2,1)} %bitcast.5, s32[4,384]{1,0:T(4,128)} %bitcast.6, s32[4,8]{1,0:T(4,128)} %bitcast.7), custom_call_target="tpu_custom_call" | custom-call | flops 3252759552 | bytes 11631816 | tf_op jit(solution)/shard_map/pallas_call | solution.py:199
  21.3 2.7 %copy.6 = f32[3,343,384]{2,1,0:T(8,128)} copy(f32[3,343,384]{2,1,0:T(8,128)} %shard_map.46) | data formatting | bytes 3161088

commit v2 on v1

--- a/solution.py
+++ b/solution.py
@@ -34,7 +34,7 @@
 def kernel(
     groups, owners, cap, first,
     mult, ops, lists, slots, out,
-    opv, mv, packf, packed, pb, y_first, y_rest, ga, gb, face_out, face_in, ghost_out, ghost_in,
+    opv, mv, packf, packed, pb, y_first, y_rest, z, g, face_out, face_in, ghost_out, ghost_in,
     op_sem, m_sem, face_send, face_recv, ghost_send, ghost_recv,
 ):
     comps, nodes, nboxes = mv.shape
@@ -42,6 +42,7 @@
     dirs = lists.shape[0]
     rest = nboxes - first
     span = y_first.shape[1] // dirs
+    table = g.shape[0] // dirs
     leaf = lax.axis_index("leaf")
     me = lax.axis_index("owner")
 
@@ -82,6 +83,14 @@
     chooser = one_hot(iota((rows, LANES), 1).astype(F32) == slot)
     low_pick = one_hot(iota((FACE, LANES), 0) == iota((FACE, LANES), 1))
     high_pick = one_hot(iota((FACE, LANES), 0) + (LANES - FACE) == iota((FACE, LANES), 1))
+
+    code = lists[...]
+    place = jnp.where(
+        code < 0, -1,
+        jnp.where(code < FACE, code + nboxes, jnp.where(code < FACE + nboxes, code - FACE, code)),
+    )
+    for d in range(dirs):
+        g[d * table:(d + 1) * table] = one_hot(iota((table, nboxes), 0) == place[d:d + 1, :])
 
     m_copy.wait()
     for c in range(comps):
@@ -124,35 +133,19 @@
 
     lax.fori_loop(1, owners, lambda k, carry: (ghost_copy(k).start(), carry)[1], 0)
 
-    code = lists[...]
-    place = jnp.where(
-        code < 0, -1,
-        jnp.where(code < FACE, code + nboxes, jnp.where(code < FACE + nboxes, code - FACE, code)),
-    )
-    for d in range(dirs):
-        row = place[d:d + 1, :]
-        ga[d] = one_hot(iota((first, nboxes), 0) == row)
-        gb[d] = one_hot(iota((gb.shape[1], nboxes), 0) + first == row)
-
-    def translate(c, weights, select):
+    def translate(c, weights, y, start):
         lhs = opv[c].reshape(span * dirs, width)
-        y = y_first if weights.shape[1] == first else y_rest
         product = jnp.dot(lhs, weights, preferred_element_type=F32)
         for t in range(y.shape[0]):
             y[t] = product[:, t * LANES:(t + 1) * LANES]
-        total = None
         for d in range(dirs):
-            part = jnp.concatenate(
-                [y[t, pl.ds(d, span, stride=dirs), :].astype(BF16) for t in range(y.shape[0])],
-                axis=1,
-            )
-            term = jnp.dot(part, select[d], preferred_element_type=F32)
-            total = term if total is None else total + term
-        return total[:nodes]
+            for t in range(y.shape[0]):
+                at = d * table + start + t * LANES
+                z[c, :span, at:at + LANES] = y[t, pl.ds(d, span, stride=dirs), :].astype(BF16)
 
     def first_pass(c, carry):
         op_copy(c).wait()
-        out[c] = translate(c, packed[:, :first], ga)
+        translate(c, packed[:, :first], y_first, 0)
         return carry
 
     lax.fori_loop(0, comps, first_pass, 0)
@@ -169,20 +162,25 @@
 
     lax.fori_loop(1, owners, lambda k, carry: (ghost_copy(k).wait(), carry)[1], 0)
 
-    pieces = [face_in[0].astype(F32), face_in[1].astype(F32)]
+    arrived = [face_in[0].astype(F32), face_in[1].astype(F32)]
     ghosts = [ghost_in[p].astype(F32) for p in range(owners)]
-    table = jnp.concatenate(pieces + ghosts, axis=0)
-    pad = gb.shape[1] - rest - table.shape[0]
+    arrived = jnp.concatenate(arrived + ghosts, axis=0)
+    pad = pb.shape[1] - rest - arrived.shape[0]
     if pad:
-        table = jnp.concatenate([table, jnp.zeros((pad, width), F32)], axis=0)
+        arrived = jnp.concatenate([arrived, jnp.zeros((pad, width), F32)], axis=0)
     pb[:, :rest] = packed[:, first:]
-    pb[:, rest:] = table.T.astype(BF16)
+    pb[:, rest:] = arrived.T.astype(BF16)
 
     def second_pass(c, carry):
-        out[c] = out[c] + translate(c, pb[...], gb)
+        translate(c, pb[...], y_rest, first)
         return carry
 
     lax.fori_loop(0, comps, second_pass, 0)
+
+    held = z.shape[1]
+    result = jnp.dot(z[...].reshape(comps * held, dirs * table), g[...], preferred_element_type=F32)
+    for c in range(comps):
+        out[c] = result[c * held:c * held + nodes]
 
 
 def local(groups, owners, multipoles, operators, lists, send_slots):
@@ -198,7 +196,7 @@
     dma = pltpu.SemaphoreType.DMA
     return pl.pallas_call(
         functools.partial(kernel, groups, owners, cap, first),
-        out_shape=jax.ShapeDtypeStruct((comps, nodes, nboxes), F32),
+        out_shape=pltpu.VMEM((comps, nodes, nboxes), F32),
         in_specs=[anywhere, anywhere, vmem, vmem],
         out_specs=vmem,
         scratch_shapes=[
@@ -209,8 +207,8 @@
             pltpu.VMEM((width, extra), BF16),
             pltpu.VMEM((first // LANES, span * dirs, LANES), F32),
             pltpu.VMEM((extra // LANES, span * dirs, LANES), F32),
-            pltpu.VMEM((dirs, first, nboxes), BF16),
-            pltpu.VMEM((dirs, extra, nboxes), BF16),
+            pltpu.VMEM((comps, round_up(nodes, 16), dirs * (first + extra)), BF16),
+            pltpu.VMEM((dirs * (first + extra), nboxes), BF16),
             pltpu.VMEM((2, FACE, width), BF16),
             pltpu.VMEM((2, FACE, width), BF16),
             pltpu.VMEM((owners, cap, width), BF16),

time: 24.2 us -> 18.6 us (0.77)
  Pallas kernels: 21.3 us -> 17.2 us
  local copies, waits for them, and re-layouts: 2.66 us -> 1.15 us
    pallas_call x1, Pallas kernels: 21.3 us -> 17.2 us  [local(): pl.pallas_call(functools.partial(kernel, groups, owners, cap, first), out...]
    unnamed x1, local copies, waits for them, and re-layouts: 2.66 us -> 1.15 us
where the time goes in v2:
time: 18.6 us; the launch traced here: 18.4 us
  Pallas kernels  17.2 us (92%)
  local copies, waits for them, and re-layouts  1.15 us (6%)
    pallas_call x1, Pallas kernels, local(): pl.pallas_call(functools.partial(kernel, groups, owners, cap, first), out...  17.2 us
    unnamed x1, local copies, waits for them, and re-layouts  1.15 us

profile of v2, /device:TPU:0, one launch (start us, length us, event | category | flops | bytes accessed | tf_op | source)
XLA Modules:
  0.0 18.4 jit_solution(1037685041642835925)
XLA Ops:
  0.0 17.2 %shard_map.46 = f32[3,343,384]{2,1,0:T(8,128)S(1)} custom-call(f32[3,343,384]{2,1,0:T(8,128)} %mult.1, bf16[1029,4,1029]{2,1,0:T(4,128)(2,1)} %bitcast.5, s32[4,384]{1,0:T(4,128)} %bitcast.6, s32[4,8]{1,0:T(4,128)} %bitcast.7), custom_call_target="tpu_custom_call" | custom-call | flops 3252759552 | bytes 11631816 | tf_op jit(solution)/shard_map/pallas_call | solution.py:197
  17.3 1.1 %copy.6 = f32[3,343,384]{2,1,0:T(8,128)} copy(f32[3,343,384]{2,1,0:T(8,128)S(1)} %shard_map.46) | data formatting | bytes 3161088

commit v3 on v2

--- a/solution.py
+++ b/solution.py
@@ -34,7 +34,7 @@
 def kernel(
     groups, owners, cap, first,
     mult, ops, lists, slots, out,
-    opv, mv, packf, packed, pb, y_first, y_rest, z, g, face_out, face_in, ghost_out, ghost_in,
+    opv, mv, packf, packed, pb, y_first, y_rest, za, zb, ga, gb, face_out, face_in, ghost_out, ghost_in,
     op_sem, m_sem, face_send, face_recv, ghost_send, ghost_recv,
 ):
     comps, nodes, nboxes = mv.shape
@@ -42,7 +42,7 @@
     dirs = lists.shape[0]
     rest = nboxes - first
     span = y_first.shape[1] // dirs
-    table = g.shape[0] // dirs
+    extra = pb.shape[1]
     leaf = lax.axis_index("leaf")
     me = lax.axis_index("owner")
 
@@ -52,8 +52,7 @@
 
     m_copy = pltpu.make_async_copy(mult, mv, m_sem)
     m_copy.start()
-    for c in range(comps):
-        op_copy(c).start()
+    op_copy(0).start()
 
     face_in[...] = jnp.zeros_like(face_in)
     ghost_in[...] = jnp.zeros_like(ghost_in)
@@ -90,9 +89,13 @@
         jnp.where(code < FACE, code + nboxes, jnp.where(code < FACE + nboxes, code - FACE, code)),
     )
     for d in range(dirs):
-        g[d * table:(d + 1) * table] = one_hot(iota((table, nboxes), 0) == place[d:d + 1, :])
+        row = place[d:d + 1, :]
+        ga[d * first:(d + 1) * first] = one_hot(iota((first, nboxes), 0) == row)
+        gb[d * extra:(d + 1) * extra] = one_hot(iota((extra, nboxes), 0) + first == row)
 
     m_copy.wait()
+    for c in range(1, comps):
+        op_copy(c).start()
     for c in range(comps):
         packf[pl.ds(c * nodes, nodes), :] = mv[c]
     packed[...] = packf[...].astype(BF16)
@@ -133,22 +136,31 @@
 
     lax.fori_loop(1, owners, lambda k, carry: (ghost_copy(k).start(), carry)[1], 0)
 
-    def translate(c, weights, y, start):
+    def translate(c, weights, y, z):
         lhs = opv[c].reshape(span * dirs, width)
         product = jnp.dot(lhs, weights, preferred_element_type=F32)
         for t in range(y.shape[0]):
             y[t] = product[:, t * LANES:(t + 1) * LANES]
         for d in range(dirs):
             for t in range(y.shape[0]):
-                at = d * table + start + t * LANES
+                at = (d * y.shape[0] + t) * LANES
                 z[c, :span, at:at + LANES] = y[t, pl.ds(d, span, stride=dirs), :].astype(BF16)
+
+    held = za.shape[1]
+
+    def gather(z, select):
+        rows = z[...].reshape(comps * held, z.shape[2])
+        return jnp.dot(rows, select[...], preferred_element_type=F32)
 
     def first_pass(c, carry):
         op_copy(c).wait()
-        translate(c, packed[:, :first], y_first, 0)
+        translate(c, packed[:, :first], y_first, za)
         return carry
 
     lax.fori_loop(0, comps, first_pass, 0)
+    gathered = gather(za, ga)
+    for c in range(comps):
+        out[c] = gathered[c * held:c * held + nodes]
 
     @pl.when(leaf < groups - 1)
     def _():
@@ -172,15 +184,14 @@
     pb[:, rest:] = arrived.T.astype(BF16)
 
     def second_pass(c, carry):
-        translate(c, pb[...], y_rest, first)
+        translate(c, pb[...], y_rest, zb)
         return carry
 
     lax.fori_loop(0, comps, second_pass, 0)
 
-    held = z.shape[1]
-    result = jnp.dot(z[...].reshape(comps * held, dirs * table), g[...], preferred_element_type=F32)
+    gathered = gather(zb, gb)
     for c in range(comps):
-        out[c] = result[c * held:c * held + nodes]
+        out[c] = out[c] + gathered[c * held:c * held + nodes]
 
 
 def local(groups, owners, multipoles, operators, lists, send_slots):
@@ -207,8 +218,10 @@
             pltpu.VMEM((width, extra), BF16),
             pltpu.VMEM((first // LANES, span * dirs, LANES), F32),
             pltpu.VMEM((extra // LANES, span * dirs, LANES), F32),
-            pltpu.VMEM((comps, round_up(nodes, 16), dirs * (first + extra)), BF16),
-            pltpu.VMEM((dirs * (first + extra), nboxes), BF16),
+            pltpu.VMEM((comps, round_up(nodes, 16), dirs * first), BF16),
+            pltpu.VMEM((comps, round_up(nodes, 16), dirs * extra), BF16),
+            pltpu.VMEM((dirs * first, nboxes), BF16),
+            pltpu.VMEM((dirs * extra, nboxes), BF16),
             pltpu.VMEM((2, FACE, width), BF16),
             pltpu.VMEM((2, FACE, width), BF16),
             pltpu.VMEM((owners, cap, width), BF16),

time: 18.6 us -> 17 us (0.914)
  Pallas kernels: 17.2 us -> 15.6 us
    pallas_call x1, Pallas kernels: 17.2 us -> 15.6 us  [local(): pl.pallas_call(functools.partial(kernel, groups, owners, cap, first), out...]
where the time goes in v3:
time: 17 us; the launch traced here: 16.8 us
  Pallas kernels  15.6 us (92%)
  local copies, waits for them, and re-layouts  1.15 us (7%)
    pallas_call x1, Pallas kernels, local(): pl.pallas_call(functools.partial(kernel, groups, owners, cap, first), out...  15.6 us
    unnamed x1, local copies, waits for them, and re-layouts  1.15 us

profile of v3, /device:TPU:0, one launch (start us, length us, event | category | flops | bytes accessed | tf_op | source)
XLA Modules:
  0.0 16.8 jit_solution(7667127406350967206)
XLA Ops:
  0.0 15.6 %shard_map.46 = f32[3,343,384]{2,1,0:T(8,128)S(1)} custom-call(f32[3,343,384]{2,1,0:T(8,128)} %mult.1, bf16[1029,4,1029]{2,1,0:T(4,128)(2,1)} %bitcast.5, s32[4,384]{1,0:T(4,128)} %bitcast.6, s32[4,8]{1,0:T(4,128)} %bitcast.7), custom_call_target="tpu_custom_call" | custom-call | flops 3252759552 | bytes 11631816 | tf_op jit(solution)/shard_map/pallas_call | solution.py:208
  15.7 1.1 %copy.6 = f32[3,343,384]{2,1,0:T(8,128)} copy(f32[3,343,384]{2,1,0:T(8,128)S(1)} %shard_map.46) | data formatting | bytes 3161088
